TPU v7x, 128 devices: a whole 4x4x4 slice. The times are simulated.
128 devices in a mesh: dp: 4 (over x), tensor: 2 (over core), expert: 16 (over z, y).
Axes of the slice: x: 4, y: 4, z: 4, core: 2. Of those that a mesh axis runs over, the one named last changes fastest.
Arguments:
- tokens: bfloat16 [8192, 2304], P(('dp', 'tensor', 'expert')), may hold values from -6 to 6
- routes: int32 [8192, 2], P(('dp', 'tensor', 'expert')), may hold values from 0 to 7, all different within a row; in each aligned block of 64 rows (0 to 63, 64 to 127, ...) at most 24 rows name the same one
- gates: float32 [8192, 2], P(('dp', 'tensor', 'expert')), may hold values from 0.2 to 1
- segments: int32 [8192], P(('dp', 'tensor', 'expert')), may hold values from 0 to 31, never falling along the last dimension, each value on 1 to 512 neighbouring positions
- w_gate: bfloat16 [16, 2304, 3840], P('expert', None, ('dp', 'tensor')), may hold values from -0.125 to 0.125
- w_up: bfloat16 [16, 2304, 3840], P('expert', None, ('dp', 'tensor')), may hold values from -0.125 to 0.125
- w_down: bfloat16 [16, 3840, 2304], P('expert', ('dp', 'tensor')), may hold values from -0.0625 to 0.0625
Outputs:
- embedded: bfloat16 [8192, 2304], P(('dp', 'tensor', 'expert'))
- pooled: float32 [32, 2304], replicated
Inputs may be any that keep to these rules, and one draw needn't show every extreme that they name: `routes`: each residue names two different experts. Within the rows of one device no expert is named more than 24 times, and in every draw some expert is named exactly 24 times by the rows of some device. `segments`: sequence numbers never fall along the residues; each sequence has 1 to 512 residues and one has exactly 512.
All inputs are finite; a program needn't handle non-finite values.
Results may differ from a plain program's by a relative error of at most 0.0085.
Values may be sent and summed in bfloat16 or wider, within the bound.
A program may use at most 64 MiB of HBM per device.

v0:
```python
import jax
import jax.numpy as jnp
from jax import lax
from jax.sharding import PartitionSpec as P

EXPERTS = 8
TOP = 2
CAP = 24
epsilon = 1e-06


def norm_tokens(tokens):
    values = tokens.astype(jnp.float32)
    scale = lax.rsqrt(jnp.mean(values * values, axis=1, keepdims=True) + epsilon)
    return (values, (values * scale).astype(jnp.bfloat16))


def slot_numbers(routes):
    flat_routes = routes.reshape(-1)
    onehot = (flat_routes[:, None] == jnp.arange(EXPERTS, dtype=jnp.int32)[None, :]).astype(
        jnp.int32
    )
    before = jnp.cumsum(onehot, axis=0) - onehot
    slot_rank = jnp.sum(before * onehot, axis=1)
    return flat_routes * CAP + slot_rank


def placement_matrix(slot_index, tok_count):
    hits = (jnp.arange(EXPERTS * CAP, dtype=jnp.int32)[:, None] == slot_index[None, :]).astype(
        jnp.int32
    )
    return jnp.sum(hits.reshape(EXPERTS * CAP, tok_count, TOP), axis=2).astype(jnp.bfloat16)


def fan_out(slot_rows, replicas):
    leading = slot_rows.shape[:-2]
    features = slot_rows.shape[-1]
    shaped = slot_rows.reshape(leading + (EXPERTS, CAP, features))
    shaped = jnp.repeat(shaped, replicas, axis=len(leading))
    return shaped.reshape(leading + (EXPERTS * replicas * CAP, features))


def expert_hidden(row_block, w_gate, w_up):
    gate_proj = jnp.einsum("nacd,adf->nacf", row_block, w_gate, preferred_element_type=jnp.float32)
    up_proj = jnp.einsum("nacd,adf->nacf", row_block, w_up, preferred_element_type=jnp.float32)
    return (jax.nn.silu(gate_proj) * up_proj).astype(jnp.bfloat16)


def shards(tokens, routes, gates, segments, w_gate, w_up, w_down):
    tok_count = tokens.shape[0]
    width = tokens.shape[1]
    experts_axis = lax.axis_size("expert")
    per_device = w_gate.shape[0]
    replicas = max(1, experts_axis // EXPERTS)
    plane = lax.axis_size("dp") * lax.axis_size("tensor")
    values, normed = norm_tokens(tokens)
    slot_index = slot_numbers(routes)
    placing = placement_matrix(slot_index, tok_count)
    slot_rows = jnp.dot(placing, normed, preferred_element_type=jnp.float32).astype(jnp.bfloat16)
    send_rows = fan_out(slot_rows, replicas)
    received = lax.all_to_all(send_rows, "expert", split_axis=0, concat_axis=0, tiled=True)
    local_rows = received.reshape(experts_axis, per_device, CAP, width)
    hidden = expert_hidden(
        lax.all_gather(local_rows, ("dp", "tensor"), axis=0, tiled=True), w_gate, w_up
    )
    summed = lax.psum_scatter(
        jnp.einsum("nacf,afd->nacd", hidden, w_down, preferred_element_type=jnp.float32).astype(
            jnp.bfloat16
        ),
        ("dp", "tensor"),
        scatter_dimension=0,
        tiled=True,
    )
    returned = lax.all_to_all(summed, "expert", split_axis=0, concat_axis=0, tiled=True).astype(
        jnp.float32
    )
    expert_out = jnp.sum(returned.reshape(EXPERTS, replicas, CAP, width), axis=1)
    picked = jnp.take(expert_out.reshape(EXPERTS * CAP, width), slot_index, axis=0).reshape(
        tok_count, TOP, width
    )
    mixed = values + jnp.sum(gates[:, :, None] * picked, axis=1)
    embedded = mixed.astype(jnp.bfloat16)
    devices_all = plane * experts_axis
    seq_total = tok_count * devices_all // 256
    seq_hot = (jnp.arange(seq_total, dtype=jnp.int32)[:, None] == segments[None, :]).astype(
        jnp.bfloat16
    )
    seq_sums = jnp.dot(seq_hot, embedded, preferred_element_type=jnp.float32)
    seq_counts = jnp.sum(seq_hot.astype(jnp.float32), axis=1)
    total_sums, total_counts = lax.psum((seq_sums, seq_counts), ("dp", "tensor", "expert"))
    pooled = total_sums / total_counts[:, None]
    return (embedded, pooled)


def solution(mesh):
    placed = (
        P(("dp", "tensor", "expert"), None),
        P(("dp", "tensor", "expert"), None),
        P(("dp", "tensor", "expert"), None),
        P(("dp", "tensor", "expert")),
        P("expert", None, ("dp", "tensor")),
        P("expert", None, ("dp", "tensor")),
        P("expert", ("dp", "tensor"), None),
    )
    return jax.shard_map(
        shards,
        mesh=mesh,
        in_specs=placed,
        out_specs=(P(("dp", "tensor", "expert"), None), P()),
        check_vma=False,
    )
```

profile of v0, /device:TPU:1, one launch (start us, length us, event | category | flops | bytes accessed | tf_op | source)
XLA Modules:
  0.0 430.2 jit_solution(17965702247409334811)
XLA Ops:
  7.2 0.9 copy.33
  8.9 0.7 compare_and_fusion
  9.7 1.1 fusion.9
  10.9 1.4 convolution_convert_fusion
  12.4 32.4 %all_to_all.14 = bf16[16,24,2304]{2,1,0:T(8,128)(2,1)S(1)} all-to-all(bf16[16,24,2304]{2,1,0:T(8,128)(2,1)S(1)} %bitcast.63), channel_id=1, replica_groups=mesh['dp'=4,'tensor'=2,'expert'=16] {'expert'}, dimensions={0} | all-to-all | bytes 3538944 | tf_op jit(solution)/shard_map/all_to_all | solution.py:61
  44.8 1.5 copy.36
  46.4 73.1 %all-gather.3.cloned.1.call-done = bf16[128,24,2304]{2,0,1:T(8,128)(2,1)} async-done(((bf16[16,24,2304]{2,0,1:T(8,128)(2,1)}), bf16[128,24,2304]{2,0,1:T(8,128)(2,1)}) %all-gather.3.cloned.1.call-update) | async-done | bytes 14155792 | tf_op jit(solution)/shard_map/all_gather | solution.py:64
  119.5 11.4 %fusion.6 = f32[128,24,480]{0,2,1:T(8,128)S(1)} fusion(bf16[128,24,2304]{2,0,1:T(8,128)(2,1)} %all-gather.3.cloned.1.call-done, bf16[1,2304,480]{1,2,0:T(8,128)(2,1)} %param.12), kind=kOutput, calls=%fused_computation.13 | convolution fusion | flops 6794772480 | bytes 22265856 | tf_op jit(solution)/shard_map/nacd,adf->nacf/dot_general | solution.py:45
  130.9 8.1 %fusion = bf16[128,1,24,480]{0,3,2,1:T(8,128)(2,1)S(1)} fusion(f32[128,24,480]{0,2,1:T(8,128)S(1)} %fusion.6, bf16[128,24,2304]{2,0,1:T(8,128)(2,1)S(1)} %copy-done.5, bf16[1,2304,480]{1,2,0:T(8,128)(2,1)S(1)} %copy-done.6), kind=kOutput, calls=%fused_computation.3 | convolution fusion | flops 6803619840 | bytes 25214976 | tf_op jit(solution)/shard_map/nacd,adf->nacf/dot_general | solution.py:44
  139.0 10.3 %convert_bitcast_fusion = bf16[128,1,24,2304]{3,0,2,1:T(8,128)(2,1)} fusion(bf16[128,1,24,480]{0,3,2,1:T(8,128)(2,1)S(1)} %fusion, bf16[1,480,2304]{2,1,0:T(8,128)(2,1)S(1)} %copy-done), kind=kOutput, calls=%fused_computation.1 | convolution fusion | flops 6801850368 | bytes 19316736 | tf_op jit(solution)/shard_map/nacf,afd->nacd/dot_general | solution.py:67
  149.3 79.5 %reduce-scatter.2.cloned.1.call-done = bf16[16,1,24,2304]{3,0,2,1:T(8,128)(2,1)} async-done(((bf16[128,1,24,2304]{3,0,2,1:T(8,128)(2,1)}), bf16[16,1,24,2304]{3,0,2,1:T(8,128)(2,1)}) %reduce-scatter.2.cloned.1.call-update) | async-done | bytes 1769488 | tf_op jit(solution)/shard_map/reduce_scatter | solution.py:66
  228.8 3.2 copy.37
  232.0 6.9 %all-to-all-start.1 = ((bf16[16,1,24,2304]{3,2,1,0:T(8,128)(2,1)}), bf16[16,1,24,2304]{3,2,1,0:T(8,128)(2,1)}, u32[]{:S(2)}, u32[]{:S(2)}) async-start(bf16[16,1,24,2304]{3,2,1,0:T(8,128)(2,1)} %copy.37), calls=%async_computation.2 | async-start | bytes 3538944 | tf_op jit(solution)/shard_map/all_to_all | solution.py:74
  238.9 0.2 all-reduce.2.cloned.1.call-start
  239.6 23.3 %all-to-all-done.1 = bf16[16,1,24,2304]{3,2,1,0:T(8,128)(2,1)} async-done(((bf16[16,1,24,2304]{3,2,1,0:T(8,128)(2,1)}), bf16[16,1,24,2304]{3,2,1,0:T(8,128)(2,1)}, u32[]{:S(2)}, u32[]{:S(2)}) %all-to-all-start.1) | async-done | bytes 1769504 | tf_op jit(solution)/shard_map/all_to_all | solution.py:74
  262.9 3.2 convert_reduce_fusion
  266.0 4.0 gather_fusion
  270.0 2.0 gather.7
  272.0 3.2 multiply_reduce_fusion
  275.3 1.0 fusion.11
  276.3 0.9 fusion.17
  277.4 68.6 %psum.15 = f32[32]{0:T(128)S(1)} all-reduce(f32[32]{0:T(128)S(1)} %convert_reduce_fusion.2), channel_id=1, replica_groups=mesh['dp'=4,'tensor'=2,'expert'=16] {'dp','tensor','expert'}, use_global_device_ids=true, to_apply=%region_9.10 | all-reduce | flops 32 | bytes 256 | tf_op jit(solution)/shard_map/psum | solution.py:90
  346.0 75.9 %all-reduce.2.cloned.1.call-done = f32[32,2304]{1,0:T(8,128)} async-done(((f32[32,2304]{1,0:T(8,128)}), f32[32,2304]{1,0:T(8,128)}) %all-reduce.2.cloned.1.call-update) | async-done | bytes 294928 | tf_op jit(solution)/shard_map/psum | solution.py:90
  421.9 1.8 broadcast_divide_fusion
  (36 shorter events, 1.7 us)
Async XLA Ops:
  7.2 131.8 %copy-start = (bf16[1,480,2304]{2,1,0:T(8,128)(2,1)S(1)}, bf16[1,480,2304]{2,1,0:T(8,128)(2,1)}, u32[]{:S(2)}) copy-start(bf16[1,480,2304]{2,1,0:T(8,128)(2,1)} %param.13) | copy-start | bytes 6635524
  7.2 112.3 %all-gather.3.cloned.1.call-start = ((), (), s32[]{:S(2)}) async-start(), calls=%async_computation.5 | async-start | bytes 15925248 | tf_op jit(solution)/shard_map/all_gather | solution.py:64
  46.3 182.4 %reduce-scatter.2.cloned.1.call-start = ((), (), s32[]{:S(2)}) async-start(), calls=%async_computation.3 | async-start | bytes 15925248 | tf_op jit(solution)/shard_map/reduce_scatter | solution.py:66
  119.5 11.4 %copy-start.5 = (bf16[128,24,2304]{2,0,1:T(8,128)(2,1)S(1)}, bf16[128,24,2304]{2,0,1:T(8,128)(2,1)}, u32[]{:S(2)}) copy-start(bf16[128,24,2304]{2,0,1:T(8,128)(2,1)} %all-gather.3.cloned.1.call-done) | copy-start | bytes 42467332
  119.5 11.4 %copy-start.6 = (bf16[1,2304,480]{1,2,0:T(8,128)(2,1)S(1)}, bf16[1,2304,480]{1,2,0:T(8,128)(2,1)}, u32[]{:S(2)}) copy-start(bf16[1,2304,480]{1,2,0:T(8,128)(2,1)} %param.11) | copy-start | bytes 6635524
  232.0 7.1 %copy-start.2 = (s32[64,2]{0,1:T(2,128)S(1)}, s32[64,2]{0,1:T(2,128)}, u32[]{:S(2)}) copy-start(s32[64,2]{0,1:T(2,128)} %param.8) | copy-start | bytes 1540
  232.0 7.5 %copy-start.3 = (f32[64,2]{0,1:T(2,128)S(1)}, f32[64,2]{0,1:T(2,128)}, u32[]{:S(2)}) copy-start(f32[64,2]{0,1:T(2,128)} %param.9) | copy-start | bytes 1540
  232.0 30.9 %all-to-all-start.1 = ((bf16[16,1,24,2304]{3,2,1,0:T(8,128)(2,1)}), bf16[16,1,24,2304]{3,2,1,0:T(8,128)(2,1)}, u32[]{:S(2)}, u32[]{:S(2)}) async-start(bf16[16,1,24,2304]{3,2,1,0:T(8,128)(2,1)} %copy.37), calls=%async_computation.2 | async-start | bytes 3538944 | tf_op jit(solution)/shard_map/all_to_all | solution.py:74
  238.9 183.0 %all-reduce.2.cloned.1.call-start = ((), (), s32[]{:S(2)}) async-start(), calls=%async_computation.4 | async-start | bytes 589824 | tf_op jit(solution)/shard_map/psum | solution.py:90
  270.0 6.3 %copy-start.4 = (s32[64]{0:T(128)S(1)}, s32[64]{0:T(128)}, u32[]{:S(2)}) copy-start(s32[64]{0:T(128)} %param.10) | copy-start | bytes 772
  276.3 147.3 %copy-start.1 = (bf16[64,2304]{1,0:T(8,128)(2,1)}, bf16[64,2304]{1,0:T(8,128)(2,1)S(1)}, u32[]{:S(2)}) copy-start(bf16[64,2304]{1,0:T(8,128)(2,1)S(1)} %fusion.11) | copy-start | bytes 884740
Sparse Core Ops, SparseCore 0:
  46.5 72.9 all-gather.2
  149.4 79.3 reduce-scatter.1
  277.4 144.4 all-reduce.1
where the time goes:
time: 431 us; the launch traced here: 430 us
  waiting for transfers between devices  252 us (58%)
  blocking collectives  101 us (23%)
  matrix products  32 us (7%)
  between operations  13.9 us (3%)
  local copies, waits for them, and re-layouts  12.5 us (3%)
  other arithmetic  11.7 us (3%)
  starting transfers between devices  7.18 us (2%)
    reduce_scatter x1, waiting for transfers between devices, shards(): lax.psum_scatter(jnp.einsum('nacf,afd->nacd', hidden, w_down, preferred_e...  79.5 us
    psum x1, waiting for transfers between devices, shards(): lax.psum((seq_sums, seq_counts), ('dp', 'tensor', 'expert'))  75.9 us
    all_gather x1, waiting for transfers between devices, shards(): lax.all_gather(local_rows, ('dp', 'tensor'), axis=0, tiled=True)  73.1 us
    psum x1, blocking collectives, shards(): lax.psum((seq_sums, seq_counts), ('dp', 'tensor', 'expert'))  68.6 us
    all_to_all x1, blocking collectives, shards(): lax.all_to_all(send_rows, 'expert', split_axis=0, concat_axis=0, tiled=True)  32.4 us
    all_to_all x1, waiting for transfers between devices, shards(): lax.all_to_all(summed, 'expert', split_axis=0, concat_axis=0, tiled=True)  23.3 us
    dot_general x1, matrix products, expert_hidden(): jnp.einsum('nacd,adf->nacf', row_block, w_up, preferred_element_type=jnp....  11.4 us
    dot_general x1, matrix products, shards(): jnp.einsum('nacf,afd->nacd', hidden, w_down, preferred_element_type=jnp.f...  10.3 us
  transfers between devices with their start and end apart: 4, of which 4 were waited for; matrix products, arithmetic and copies ran while one was open for 0% of the time, Pallas kernels for 0%

commit v1 on v0

--- a/solution.py
+++ b/solution.py
@@ -87,7 +87,9 @@
     )
     seq_sums = jnp.dot(seq_hot, embedded, preferred_element_type=jnp.float32)
     seq_counts = jnp.sum(seq_hot.astype(jnp.float32), axis=1)
-    total_sums, total_counts = lax.psum((seq_sums, seq_counts), ("dp", "tensor", "expert"))
+    total_sums, total_counts = lax.psum(
+        lax.psum((seq_sums, seq_counts), ("tensor", "expert")), "dp"
+    )
     pooled = total_sums / total_counts[:, None]
     return (embedded, pooled)
 

time: 431 us -> 464 us (1.077)
  waiting for transfers between devices: 252 us -> 279 us
  blocking collectives: 101 us -> 106 us
    psum x1 -> x2, waiting for transfers between devices: 75.9 us -> 103 us  [the longest x1 103 us: shards(): lax.psum((seq_sums, seq_counts), ('tensor', 'expert'))]
    psum x1 -> x2, blocking collectives: 68.6 us -> 73.6 us  [the longest x1 65.2 us: shards(): lax.psum((seq_sums, seq_counts), ('tensor', 'expert'))]
  transfers between devices with their start and end apart: 4 -> 5, of which waited for: 4 -> 4; matrix products, arithmetic and copies ran while one was open for 0% -> 0% of each run, Pallas kernels for 0% -> 0%
where the time goes in v1:
time: 464 us; the launch traced here: 463 us
  waiting for transfers between devices  279 us (60%)
  blocking collectives  106 us (23%)
  matrix products  32 us (7%)
  between operations  13.9 us (3%)
  local copies, waits for them, and re-layouts  12.5 us (3%)
  other arithmetic  11.7 us (3%)
  starting transfers between devices  7.22 us (2%)
    psum x1, waiting for transfers between devices, shards(): lax.psum((seq_sums, seq_counts), ('tensor', 'expert'))  103 us
    reduce_scatter x1, waiting for transfers between devices, shards(): lax.psum_scatter(jnp.einsum('nacf,afd->nacd', hidden, w_down, preferred_e...  79.5 us
    all_gather x1, waiting for transfers between devices, shards(): lax.all_gather(local_rows, ('dp', 'tensor'), axis=0, tiled=True)  73.1 us
    psum x1, blocking collectives, shards(): lax.psum((seq_sums, seq_counts), ('tensor', 'expert'))  65.2 us
    all_to_all x1, blocking collectives, shards(): lax.all_to_all(send_rows, 'expert', split_axis=0, concat_axis=0, tiled=True)  32.4 us
    all_to_all x1, waiting for transfers between devices, shards(): lax.all_to_all(summed, 'expert', split_axis=0, concat_axis=0, tiled=True)  23.3 us
    dot_general x1, matrix products, expert_hidden(): jnp.einsum('nacd,adf->nacf', row_block, w_up, preferred_element_type=jnp....  11.4 us
    dot_general x1, matrix products, shards(): jnp.einsum('nacf,afd->nacd', hidden, w_down, preferred_element_type=jnp.f...  10.3 us
  transfers between devices with their start and end apart: 5, of which 4 were waited for; matrix products, arithmetic and copies ran while one was open for 0% of the time, Pallas kernels for 0%

profile of v1, /device:TPU:1, one launch (start us, length us, event | category | flops | bytes accessed | tf_op | source)
XLA Modules:
  0.0 462.6 jit_solution(10304949479997304441)
XLA Ops:
  7.2 0.9 copy.33
  8.9 0.7 compare_and_fusion
  9.7 1.1 fusion.9
  10.9 1.4 convolution_convert_fusion
  12.4 32.4 %all_to_all.14 = bf16[16,24,2304]{2,1,0:T(8,128)(2,1)S(1)} all-to-all(bf16[16,24,2304]{2,1,0:T(8,128)(2,1)S(1)} %bitcast.63), channel_id=1, replica_groups=mesh['dp'=4,'tensor'=2,'expert'=16] {'expert'}, dimensions={0} | all-to-all | bytes 3538944 | tf_op jit(solution)/shard_map/all_to_all | solution.py:61
  44.8 1.5 copy.36
  46.4 73.1 %all-gather.3.cloned.1.call-done = bf16[128,24,2304]{2,0,1:T(8,128)(2,1)} async-done(((bf16[16,24,2304]{2,0,1:T(8,128)(2,1)}), bf16[128,24,2304]{2,0,1:T(8,128)(2,1)}) %all-gather.3.cloned.1.call-update) | async-done | bytes 14155792 | tf_op jit(solution)/shard_map/all_gather | solution.py:64
  119.5 11.4 %fusion.6 = f32[128,24,480]{0,2,1:T(8,128)S(1)} fusion(bf16[128,24,2304]{2,0,1:T(8,128)(2,1)} %all-gather.3.cloned.1.call-done, bf16[1,2304,480]{1,2,0:T(8,128)(2,1)} %param.12), kind=kOutput, calls=%fused_computation.13 | convolution fusion | flops 6794772480 | bytes 22265856 | tf_op jit(solution)/shard_map/nacd,adf->nacf/dot_general | solution.py:45
  130.9 8.1 %fusion = bf16[128,1,24,480]{0,3,2,1:T(8,128)(2,1)S(1)} fusion(f32[128,24,480]{0,2,1:T(8,128)S(1)} %fusion.6, bf16[128,24,2304]{2,0,1:T(8,128)(2,1)S(1)} %copy-done.5, bf16[1,2304,480]{1,2,0:T(8,128)(2,1)S(1)} %copy-done.6), kind=kOutput, calls=%fused_computation.3 | convolution fusion | flops 6803619840 | bytes 25214976 | tf_op jit(solution)/shard_map/nacd,adf->nacf/dot_general | solution.py:44
  139.0 10.3 %convert_bitcast_fusion = bf16[128,1,24,2304]{3,0,2,1:T(8,128)(2,1)} fusion(bf16[128,1,24,480]{0,3,2,1:T(8,128)(2,1)S(1)} %fusion, bf16[1,480,2304]{2,1,0:T(8,128)(2,1)S(1)} %copy-done), kind=kOutput, calls=%fused_computation.1 | convolution fusion | flops 6801850368 | bytes 19316736 | tf_op jit(solution)/shard_map/nacf,afd->nacd/dot_general | solution.py:67
  149.3 79.5 %reduce-scatter.2.cloned.1.call-done = bf16[16,1,24,2304]{3,0,2,1:T(8,128)(2,1)} async-done(((bf16[128,1,24,2304]{3,0,2,1:T(8,128)(2,1)}), bf16[16,1,24,2304]{3,0,2,1:T(8,128)(2,1)}) %reduce-scatter.2.cloned.1.call-update) | async-done | bytes 1769488 | tf_op jit(solution)/shard_map/reduce_scatter | solution.py:66
  228.8 3.2 copy.37
  232.0 6.9 %all-to-all-start.1 = ((bf16[16,1,24,2304]{3,2,1,0:T(8,128)(2,1)}), bf16[16,1,24,2304]{3,2,1,0:T(8,128)(2,1)}, u32[]{:S(2)}, u32[]{:S(2)}) async-start(bf16[16,1,24,2304]{3,2,1,0:T(8,128)(2,1)} %copy.37), calls=%async_computation.2 | async-start | bytes 3538944 | tf_op jit(solution)/shard_map/all_to_all | solution.py:74
  239.6 23.3 %all-to-all-done.1 = bf16[16,1,24,2304]{3,2,1,0:T(8,128)(2,1)} async-done(((bf16[16,1,24,2304]{3,2,1,0:T(8,128)(2,1)}), bf16[16,1,24,2304]{3,2,1,0:T(8,128)(2,1)}, u32[]{:S(2)}, u32[]{:S(2)}) %all-to-all-start.1) | async-done | bytes 1769504 | tf_op jit(solution)/shard_map/all_to_all | solution.py:74
  262.9 3.2 convert_reduce_fusion
  266.0 4.0 gather_fusion
  270.0 2.0 gather.7
  272.0 3.2 multiply_reduce_fusion
  275.3 1.0 fusion.11
  276.3 0.9 fusion.17
  277.3 103.3 %all-reduce.3.cloned.1.call-done = f32[32,2304]{1,0:T(8,128)} async-done(((f32[32,2304]{1,0:T(8,128)}), f32[32,2304]{1,0:T(8,128)}) %all-reduce.3.cloned.1.call-update) | async-done | bytes 294928 | tf_op jit(solution)/shard_map/psum | solution.py:91
  380.7 65.2 %psum.30 = f32[32]{0:T(128)S(1)} all-reduce(f32[32]{0:T(128)S(1)} %convert_reduce_fusion.2), channel_id=1, replica_groups=mesh['dp'=4,'tensor'=2,'expert'=16] {'tensor','expert'}, use_global_device_ids=true, to_apply=%region_10.11 | all-reduce | flops 32 | bytes 256 | tf_op jit(solution)/shard_map/psum | solution.py:91
  445.9 8.4 %psum.31 = f32[32]{0:T(128)S(1)} all-reduce(f32[32]{0:T(128)S(1)} %psum.30), channel_id=1, replica_groups=mesh['dp'=4,'tensor'=2,'expert'=16] {'dp'}, use_global_device_ids=true, to_apply=%region_11.12 | all-reduce | flops 32 | bytes 256 | tf_op jit(solution)/shard_map/psum | solution.py:90
  454.3 1.8 broadcast_divide_fusion
  (40 shorter events, 2.0 us)
Async XLA Ops:
  7.2 131.8 %copy-start = (bf16[1,480,2304]{2,1,0:T(8,128)(2,1)S(1)}, bf16[1,480,2304]{2,1,0:T(8,128)(2,1)}, u32[]{:S(2)}) copy-start(bf16[1,480,2304]{2,1,0:T(8,128)(2,1)} %param.13) | copy-start | bytes 6635524
  7.2 112.3 %all-gather.3.cloned.1.call-start = ((), (), s32[]{:S(2)}) async-start(), calls=%async_computation.6 | async-start | bytes 15925248 | tf_op jit(solution)/shard_map/all_gather | solution.py:64
  46.3 182.4 %reduce-scatter.2.cloned.1.call-start = ((), (), s32[]{:S(2)}) async-start(), calls=%async_computation.3 | async-start | bytes 15925248 | tf_op jit(solution)/shard_map/reduce_scatter | solution.py:66
  119.5 11.4 %copy-start.5 = (bf16[128,24,2304]{2,0,1:T(8,128)(2,1)S(1)}, bf16[128,24,2304]{2,0,1:T(8,128)(2,1)}, u32[]{:S(2)}) copy-start(bf16[128,24,2304]{2,0,1:T(8,128)(2,1)} %all-gather.3.cloned.1.call-done) | copy-start | bytes 42467332
  119.5 11.4 %copy-start.6 = (bf16[1,2304,480]{1,2,0:T(8,128)(2,1)S(1)}, bf16[1,2304,480]{1,2,0:T(8,128)(2,1)}, u32[]{:S(2)}) copy-start(bf16[1,2304,480]{1,2,0:T(8,128)(2,1)} %param.11) | copy-start | bytes 6635524
  232.0 7.1 %copy-start.2 = (s32[64,2]{0,1:T(2,128)S(1)}, s32[64,2]{0,1:T(2,128)}, u32[]{:S(2)}) copy-start(s32[64,2]{0,1:T(2,128)} %param.8) | copy-start | bytes 1540
  232.0 7.5 %copy-start.3 = (f32[64,2]{0,1:T(2,128)S(1)}, f32[64,2]{0,1:T(2,128)}, u32[]{:S(2)}) copy-start(f32[64,2]{0,1:T(2,128)} %param.9) | copy-start | bytes 1540
  232.0 30.9 %all-to-all-start.1 = ((bf16[16,1,24,2304]{3,2,1,0:T(8,128)(2,1)}), bf16[16,1,24,2304]{3,2,1,0:T(8,128)(2,1)}, u32[]{:S(2)}, u32[]{:S(2)}) async-start(bf16[16,1,24,2304]{3,2,1,0:T(8,128)(2,1)} %copy.37), calls=%async_computation.2 | async-start | bytes 3538944 | tf_op jit(solution)/shard_map/all_to_all | solution.py:74
  238.9 141.7 %all-reduce.3.cloned.1.call-start = ((), (), s32[]{:S(2)}) async-start(), calls=%async_computation.4 | async-start | bytes 589824 | tf_op jit(solution)/shard_map/psum | solution.py:91
  270.0 6.3 %copy-start.4 = (s32[64]{0:T(128)S(1)}, s32[64]{0:T(128)}, u32[]{:S(2)}) copy-start(s32[64]{0:T(128)} %param.10) | copy-start | bytes 772
  276.3 179.8 %copy-start.1 = (bf16[64,2304]{1,0:T(8,128)(2,1)}, bf16[64,2304]{1,0:T(8,128)(2,1)S(1)}, u32[]{:S(2)}) copy-start(bf16[64,2304]{1,0:T(8,128)(2,1)S(1)} %fusion.11) | copy-start | bytes 884740
  277.2 177.1 %all-reduce.5.cloned.1.call-start = ((), (), s32[]{:S(2)}) async-start(), calls=%async_computation.5 | async-start | bytes 589824 | tf_op jit(solution)/shard_map/psum | solution.py:90
Sparse Core Ops, SparseCore 0:
  46.5 72.9 all-gather.2
  149.4 79.3 reduce-scatter.1
  277.4 103.1 all-reduce.2
  382.8 39.3 all-reduce.4
